TPU v7x, 256 devices: a whole 4x4x8 slice. The times are simulated.
256 devices in a mesh: dp: 64 (over z, x, core), mp: 4 (over y).
Axes of the slice: x: 4, y: 4, z: 8, core: 2. Of those that a mesh axis runs over, the one named last changes fastest.
Arguments:
- grads: bfloat16 [2, 4096, 8192], P(None, 'dp', 'mp'), may hold values from -6 to 6
- weights: bfloat16 [2, 4096, 8192], P(None, 'dp', 'mp'), may hold values from -6 to 6
- slot_block: int32 [64], replicated, may hold values from 0 to 63, each once
- first_moment: float32 [4, 64, 512, 512], P('mp', 'dp'), may hold values from -100 to 100
- second_moment: float32 [4, 64, 512, 512], P('mp', 'dp'), may hold values from 0.05 to 2
- left_stats: float32 [4, 64, 512, 512], P('mp', 'dp'), as said below
- right_stats: float32 [4, 64, 512, 512], P('mp', 'dp'), as said below
- left_basis: bfloat16 [4, 64, 512, 512], P('mp', 'dp'), as said below
- right_basis: bfloat16 [4, 64, 512, 512], P('mp', 'dp'), as said below
Outputs:
- step_update: bfloat16 [2, 4096, 8192], P(None, 'dp', 'mp')
- first_next: float32 [4, 64, 512, 512], P('mp', 'dp')
- second_next: float32 [4, 64, 512, 512], P('mp', 'dp')
- left_next: float32 [4, 64, 512, 512], P('mp', 'dp')
- right_next: float32 [4, 64, 512, 512], P('mp', 'dp')
- left_basis_next: bfloat16 [4, 64, 512, 512], P('mp', 'dp')
- right_basis_next: bfloat16 [4, 64, 512, 512], P('mp', 'dp')
Inputs may be any that keep to these rules, and one draw needn't show every extreme that they name: `slot_block`: each of the 64 block numbers appears once; slot s is kept on the dp device of index s. `left_stats`: symmetric with a dominant positive diagonal. `right_stats`: symmetric with a dominant positive diagonal. `left_basis`: each block is an orthogonal matrix plus a small perturbation. `right_basis`: each block is an orthogonal matrix plus a small perturbation.
All inputs are finite; a program needn't handle non-finite values.
Results may differ from a plain program's by a relative error of at most 0.015.
Values may be sent and summed in bfloat16 or wider, within the bound.
A program may use at most 64 MiB of HBM per device.

v0:
```python
import functools

import jax
import jax.numpy as jnp
from jax import lax
from jax.experimental import pallas as pl
from jax.experimental.pallas import tpu as pltpu
from jax.sharding import PartitionSpec as P

D = 4096
QW = 8192
MATS = 2
NS_STEPS = 2
beta_one = 0.9
beta_two = 0.95
stat_decay = 0.95
adam_eps = 1e-08
clip_rms = 0.2
decay_weight = 0.2
first_fix = 1.0 - 0.9**10
second_fix = 1.0 - 0.95**10
margin = 1.25

MESH = pl.DeviceIdType.MESH
F32 = jnp.float32
BF16 = jnp.bfloat16
SLAB = 8


def mm(a, b):
    return jnp.dot(a, b, preferred_element_type=F32)


def mm_t(a, b):
    return lax.dot_general(a, b, (((1,), (1,)), ((), ())), preferred_element_type=F32)


def orthogonalize(products):
    currents = []
    for product in products:
        norm_value = jnp.sqrt(jnp.sum(product * product) + 1e-12)
        factor = float(product.shape[0]) ** 0.5 / margin
        currents.append((product * (factor / norm_value)).astype(BF16))
    for turn in range(NS_STEPS):
        squares = [mm_t(x, x).astype(BF16) for x in currents]
        moved = [mm(s, x) for s, x in zip(squares, currents)]
        currents = [
            (1.5 * x.astype(F32) - 0.5 * m).astype(BF16) for x, m in zip(currents, moved)
        ]
    return currents


def far_first(zs):
    return sorted(range(zs), key=lambda j: (abs(2 * j - zs), j))


def all_of(ref, count, sem):
    part = ref.at[pl.ds(0, count)]
    return pltpu.make_async_copy(part, part, sem)


def exchange_kernel(
    n,
    groups,
    dims,
    slot_hbm,
    grads_hbm,
    weights_hbm,
    first_hbm,
    second_hbm,
    left_hbm,
    right_hbm,
    lbasis_hbm,
    rbasis_hbm,
    first_out,
    second_out,
    left_out,
    right_out,
    lnext_out,
    rnext_out,
    ubuf,
    onehot_t,
    weights,
    totals,
    slot,
    grads,
    first,
    second,
    left,
    right,
    lbasis,
    rbasis,
    onehot,
    lbasis_t,
    gsend,
    gbuf,
    usend,
    parts,
    mate_sem,
    load_sem,
    grad_sem,
    gsend_sem,
    grecv_sem,
    usend_sem,
    urecv_sem,
    psend_sem,
    precv_sem,
    tsend_sem,
    trecv_sem,
):
    mats, block_rows, block_cols, width = dims
    side = n * SLAB
    stripe = mats * block_rows * SLAB
    me = lax.axis_index("dp")
    mine = lax.axis_index("mp")
    xs = 4 if n >= 8 else 1
    zs = n // (2 * xs)
    plane = lax.div(me, 2 * xs)
    x = lax.rem(lax.div(me, 2), xs)
    core = lax.rem(me, 2)
    planes = [lax.rem(plane + i, zs) * (2 * xs) for i in range(zs)]
    columns = [lax.rem(x + i, xs) * 2 for i in range(xs)]

    def hops(i, j):
        return min(i, xs - i) + min(j, zs - j)

    spread = sorted(((i, j) for i in range(xs) for j in range(zs)), key=lambda p: -hops(*p))

    def fan_out(start, places):
        for c, i, j in places:
            if i or j:
                start(planes[j] + columns[i] + c)
            else:
                pl.when(core != c)(functools.partial(start, planes[j] + columns[i] + c))


    sheet = [
        (planes[0] + columns[i] + 1, lax.rem(mine + j, groups))
        for j in range(groups)
        for i in range(xs)
    ]
    pillar = [planes[j] + columns[0] + c for j in far_first(zs) for c in (1, 0) if j or not c]
    barrier = pltpu.get_barrier_semaphore()

    def greet(dp, mp):
        pl.semaphore_signal(barrier, inc=1, device_id=(dp, mp), device_id_type=MESH)

    near = [p for p in spread if min(p[1], zs - p[1]) <= min(1, zs // 2 - 1)]
    far = [p for p in spread if p not in near]
    for i, j in far:
        greet(planes[j] + columns[i], mine)
    for i, j in near:
        if i or j:
            greet(planes[j] + columns[i] + 1, mine)
    pl.when(core == 0)(functools.partial(greet, me + 1, mine))

    @pl.when(core == 1)
    def _():
        greet(me - 1, mine)
        for k, (there, group) in enumerate(sheet):
            if k >= xs:
                greet(there - 1, group)

    pairs = [
        (slot_hbm, slot),
        (lbasis_hbm, lbasis),
        (rbasis_hbm, rbasis),
        (first_hbm, first),
        (second_hbm, second),
        (left_hbm, left),
        (right_hbm, right),
        (weights_hbm, weights),
    ]
    loads = [pltpu.make_async_copy(a, b, load_sem.at[i]) for i, (a, b) in enumerate(pairs)]
    per_col = mats * block_rows
    grad_loads = [
        pltpu.make_async_copy(
            grads_hbm.at[:, :, pl.ds(c * width, width)],
            grads.at[pl.ds(c * per_col, per_col)],
            grad_sem.at[c],
        )
        for c in range(block_cols)
    ]
    loads[0].start()
    for load in grad_loads:
        load.start()

    loads[0].wait()
    for load in grad_loads:
        load.wait()
    for load in loads[1:]:
        load.start()

    def stage(s, carry):
        block = slot[s]
        c = lax.rem(block, block_cols)
        rest = lax.div(block, block_cols)
        gsend[s] = grads[c * per_col + rest]
        return carry

    lax.fori_loop(0, n, stage, 0, unroll=4)

    def send_grad(peer):
        pltpu.make_async_remote_copy(
            src_ref=gsend.at[peer],
            dst_ref=gbuf.at[me],
            send_sem=gsend_sem,
            recv_sem=grecv_sem,
            device_id=(peer, mine),
            device_id_type=MESH,
        ).start()

    def tell_mate():
        pl.semaphore_signal(
            mate_sem, inc=1, device_id=(me + 1 - 2 * core, mine), device_id_type=MESH
        )

    @pl.when(core == 1)
    def _():
        pl.semaphore_wait(barrier, 2 * len(near) - 1)
        tell_mate()

    pl.when(core == 0)(lambda: pl.semaphore_wait(mate_sem, 1))
    fan_out(send_grad, [(c, i, j) for c in (1, 0) for i, j in near])

    @pl.when(core == 0)
    def _():
        pl.semaphore_wait(barrier, 2 * len(far) + 1 + (groups - 1) * xs)
        tell_mate()

    pl.when(core == 1)(lambda: pl.semaphore_wait(mate_sem, 1))
    fan_out(send_grad, [(c, i, j) for c in (1, 0) for i, j in far])
    gbuf[me] = gsend[me]

    lanes = lax.broadcasted_iota(jnp.int32, (SLAB, side), 1)
    rows = lax.broadcasted_iota(jnp.int32, (SLAB, side), 0)

    def pick(s, carry):
        block = slot[s]
        c = lax.rem(block, block_cols)
        rest = lax.div(block, block_cols)
        base = c * stripe + rest * SLAB
        onehot[s] = (lanes - rows == base).astype(F32)
        return carry

    lax.fori_loop(0, n, pick, 0)
    onehot_t[...] = onehot[...].reshape(side, side).T.astype(BF16)
    loads[1].wait()
    lbasis_t[...] = lbasis[...].reshape(side, side).T

    for load in loads[2:5]:
        load.wait()

    all_of(gbuf, n - 1, grecv_sem).wait()
    grad = gbuf[...].reshape(side, width)
    half = mm(lbasis_t[...], grad).astype(BF16)
    rotated = mm(half, rbasis[...])
    new_first = beta_one * first[...] + (1.0 - beta_one) * rotated
    new_second = beta_two * second[...] + (1.0 - beta_two) * rotated * rotated
    first_out[...] = new_first
    second_out[...] = new_second
    normal = (new_first / first_fix / (jnp.sqrt(new_second / second_fix) + adam_eps)).astype(BF16)
    back = mm(lbasis[...].reshape(side, side), normal).astype(BF16)

    def send_update(peer):
        pltpu.make_async_remote_copy(
            src_ref=usend.at[peer],
            dst_ref=ubuf.at[me],
            send_sem=usend_sem,
            recv_sem=urecv_sem,
            device_id=(peer, mine),
            device_id_type=MESH,
        ).start()

    update = mm_t(back, rbasis[...]).astype(BF16)
    usend[...] = update.reshape(n, SLAB, width)
    wide = update.astype(F32)
    part = jnp.sum(wide * wide, axis=0, keepdims=True)
    lanes = sum(part[:, i * 128 : (i + 1) * 128] for i in range(width // 128))
    spot = (mine * xs + x) * 2 + core
    parts[spot] = lanes

    def send_part(there):
        pltpu.make_async_remote_copy(
            src_ref=parts.at[spot],
            dst_ref=parts.at[spot],
            send_sem=psend_sem,
            recv_sem=precv_sem,
            device_id=there,
            device_id_type=MESH,
        ).start()

    for k in sorted(range(1, len(sheet)), key=lambda k: -hops(k % xs, 0) - min(k // xs, groups - k // xs)):
        send_part(sheet[k])
    pl.when(core == 0)(functools.partial(send_part, sheet[0]))
    fan_out(send_update, [(c, i, j) for i in range(xs) for j in far_first(zs) for c in (1, 0)])
    ubuf[me] = usend[me]

    loads[5].wait()
    loads[6].wait()
    new_left = stat_decay * left[...] + (1.0 - stat_decay) * mm_t(grad, grad)
    left_out[...] = new_left
    new_right = stat_decay * right[...] + (1.0 - stat_decay) * mm(grad.T, grad)
    right_out[...] = new_right

    left_new, right_new = orthogonalize(
        [
            mm(left_out[...].astype(BF16), lbasis[...].reshape(side, side)),
            mm(right_out[...].astype(BF16), rbasis[...]),
        ]
    )
    lnext_out[...] = left_new
    rnext_out[...] = right_new

    @pl.when(core == 1)
    def _():
        all_of(parts, 2 * len(sheet) - 1, precv_sem).wait()
        totals[plane] = jnp.sum(parts[...], axis=0)
        for there in pillar:
            pltpu.make_async_remote_copy(
                src_ref=totals.at[plane],
                dst_ref=totals.at[plane],
                send_sem=tsend_sem,
                recv_sem=trecv_sem,
                device_id=(there, mine),
                device_id_type=MESH,
            ).start()
        all_of(totals, zs - 1, trecv_sem).wait()

    @pl.when(core == 0)
    def _():
        all_of(totals, zs, trecv_sem).wait()

    loads[7].wait()
    all_of(gsend, n - 1, gsend_sem).wait()
    all_of(usend, n - 1, usend_sem).wait()

    all_of(parts, len(sheet) - 1, psend_sem).wait()

    @pl.when(core == 1)
    def _():
        all_of(parts, len(pillar), tsend_sem).wait()

    @pl.when(core == 0)
    def _():
        all_of(parts, 1, psend_sem).wait()

    all_of(ubuf, n - 1, urecv_sem).wait()


def store_kernel(dims, *refs):
    mats, block_rows, block_cols, width = dims
    stripe = mats * block_rows * SLAB
    done, (ubuf, onehot_t, weights, totals), rest = refs[:6], refs[6:10], refs[10:]
    step_hbm, outs, (step, sems) = rest[0], rest[1:7], rest[7:]
    copies = [pltpu.make_async_copy(a, b, sems.at[i]) for i, (a, b) in enumerate(zip(done, outs))]
    for copy in copies:
        copy.start()
    n = ubuf.shape[0]
    total = jnp.sum(totals[...])
    scale = jnp.minimum(1.0, clip_rms / jnp.sqrt(total / float(MATS * D * QW) + 1e-12))
    returned = ubuf[...].reshape(n * SLAB, width)
    for c in range(block_cols):
        placed = mm(onehot_t[c * stripe : (c + 1) * stripe, :], returned)
        at = slice(c * width, (c + 1) * width)
        step[:, at] = (scale * placed + decay_weight * weights[:, at].astype(F32)).astype(BF16)
    last = pltpu.make_async_copy(step, step_hbm, sems.at[6])
    last.start()
    for copy in copies:
        copy.wait()
    last.wait()


def body(n, groups, grads, weights, slot_block, first, second, left, right, lbasis, rbasis):
    mats, rows, cols = grads.shape
    side, width = first.shape[-2:]
    block_rows = rows // SLAB
    block_cols = cols // width
    dims = (mats, block_rows, block_cols, width)
    vmem = pltpu.VMEM
    xs = 4 if n >= 8 else 1
    zs = n // (2 * xs)
    dma = pltpu.SemaphoreType.DMA
    flat = (mats * rows, cols)
    shape = jax.ShapeDtypeStruct
    owned = [
        shape((side, width), F32),
        shape((side, width), F32),
        shape((side, side), F32),
        shape((width, width), F32),
        shape((side, side), BF16),
        shape((width, width), BF16),
    ]
    passed = [
        shape((n, SLAB, width), BF16),
        shape((side, side), BF16),
        shape(flat, BF16),
        shape((zs, 1, 128), F32),
    ]
    here = pl.BlockSpec(memory_space=pltpu.VMEM)
    away = pl.BlockSpec(memory_space=pltpu.HBM)
    results = pl.pallas_call(
        functools.partial(exchange_kernel, n, groups, dims),
        out_shape=owned + passed,
        in_specs=[away] * 9,
        out_specs=[here] * 10,
        scratch_shapes=[
            pltpu.SMEM((n,), jnp.int32),
            vmem((n, SLAB, width), BF16),
            vmem((side, width), F32),
            vmem((side, width), F32),
            vmem((side, side), F32),
            vmem((width, width), F32),
            vmem((n, SLAB, side), BF16),
            vmem((width, width), BF16),
            vmem((n, SLAB, side), F32),
            vmem((side, side), BF16),
            vmem((n, SLAB, width), BF16),
            vmem((n, SLAB, width), BF16),
            vmem((n, SLAB, width), BF16),
            vmem((2 * groups * xs, 1, 128), F32),
            pltpu.SemaphoreType.REGULAR,
            dma((8,)),
            dma((block_cols,)),
            dma,
            dma,
            dma,
            dma,
            dma,
            dma,
            dma,
            dma,
        ],
        compiler_params=pltpu.CompilerParams(
            collective_id=0, has_side_effects=True, vmem_limit_bytes=40 * 1024 * 1024
        ),
    )(
        *[
            pltpu.with_memory_space_constraint(x, pltpu.HBM)
            for x in (
                slot_block,
                grads.reshape(mats * block_rows, SLAB, cols),
                weights.reshape(flat),
                first[0, 0],
                second[0, 0],
                left[0, 0],
                right[0, 0],
                lbasis[0, 0].reshape(n, SLAB, side),
                rbasis[0, 0],
            )
        ]
    )
    stored = pl.pallas_call(
        functools.partial(store_kernel, dims),
        out_shape=[shape(flat, BF16)] + owned,
        in_specs=[here] * 10,
        out_specs=[away] * 7,
        scratch_shapes=[vmem(flat, BF16), dma((7,))],
        compiler_params=pltpu.CompilerParams(vmem_limit_bytes=40 * 1024 * 1024),
    )(*results)
    return (stored[0].reshape(grads.shape), *[r[None, None] for r in stored[1:]])


def solution(mesh):
    owned = P("mp", "dp", None, None)
    rows = P(None, "dp", "mp")
    return jax.shard_map(
        functools.partial(body, mesh.shape["dp"], mesh.shape["mp"]),
        mesh=mesh,
        in_specs=(rows, rows, P()) + (owned,) * 6,
        out_specs=(rows,) + (owned,) * 6,
        check_vma=False,
    )
```

profile of v0, /device:TPU:16, one launch (start us, length us, event | category | flops | bytes accessed | tf_op | source)
XLA Modules:
  0.0 40.0 jit_solution(11268864286130389572)
XLA Ops:
  0.6 36.8 %shard_map.144 = (f32[512,512]{1,0:T(8,128)S(1)}, f32[512,512]{1,0:T(8,128)S(1)}, f32[512,512]{1,0:T(8,128)S(1)}, f32[512,512]{1,0:T(8,128)S(1)}, bf16[512,512]{...) custom-call(s32[64]{0:T(128)} %slot_hbm.1, ...), custom_call_target="tpu_custom_call" | custom-call | tf_op jit(solution)/shard_map/pallas_call | solution.py:402
  37.4 2.6 %shard_map.145 = (bf16[128,2048]{1,0:T(8,128)(2,1)}, f32[512,512]{1,0:T(8,128)}, f32[512,512]{1,0:T(8,128)}, f32[512,512]{1,0:T(8,128)}, f32[512,512]{1,0:T(8,12...) custom-call(f32[512,512]{1,0:T(8,128)S(1)} %get-tuple-element.24.refs_0_, ...), custom_call_target="tpu_custom_call" | custom-call | tf_op jit(solution)/shard_map/pallas_call | solution.py:453
where the time goes:
time: 40.1 us; the launch traced here: 40 us
  Pallas kernels  39.3 us (98%)
  between operations  0.64 us (2%)
    pallas_call x1, Pallas kernels, body(): pl.pallas_call(functools.partial(exchange_kernel, n, groups, dims), out_s...  36.8 us
    pallas_call x1, Pallas kernels, body(): pl.pallas_call(functools.partial(store_kernel, dims), out_shape=[shape(fl...  2.56 us

commit v1 on v0

--- a/solution.py
+++ b/solution.py
@@ -293,7 +293,7 @@
     for k in sorted(range(1, len(sheet)), key=lambda k: -hops(k % xs, 0) - min(k // xs, groups - k // xs)):
         send_part(sheet[k])
     pl.when(core == 0)(functools.partial(send_part, sheet[0]))
-    fan_out(send_update, [(c, i, j) for i in range(xs) for j in far_first(zs) for c in (1, 0)])
+    fan_out(send_update, [(c, i, j) for i in sorted(range(xs), key=lambda i: -min(i, xs - i)) for j in far_first(zs) for c in (1, 0)])
     ubuf[me] = usend[me]
 
     loads[5].wait()

time: 40.1 us -> 40 us (level)
  no operation moved by 1% of the time
where the time goes in v1:
time: 40 us; the launch traced here: 39.9 us
  Pallas kernels  39.3 us (98%)
  between operations  0.64 us (2%)
    pallas_call x1, Pallas kernels, body(): pl.pallas_call(functools.partial(exchange_kernel, n, groups, dims), out_s...  36.7 us
    pallas_call x1, Pallas kernels, body(): pl.pallas_call(functools.partial(store_kernel, dims), out_shape=[shape(fl...  2.56 us

profile of v1, /device:TPU:16, one launch (start us, length us, event | category | flops | bytes accessed | tf_op | source)
XLA Modules:
  0.0 39.9 jit_solution(13609918615370021428)
XLA Ops:
  0.6 36.7 %shard_map.144 = (f32[512,512]{1,0:T(8,128)S(1)}, f32[512,512]{1,0:T(8,128)S(1)}, f32[512,512]{1,0:T(8,128)S(1)}, f32[512,512]{1,0:T(8,128)S(1)}, bf16[512,512]{...) custom-call(s32[64]{0:T(128)} %slot_hbm.1, ...), custom_call_target="tpu_custom_call" | custom-call | tf_op jit(solution)/shard_map/pallas_call | solution.py:402
  37.4 2.6 %shard_map.145 = (bf16[128,2048]{1,0:T(8,128)(2,1)}, f32[512,512]{1,0:T(8,128)}, f32[512,512]{1,0:T(8,128)}, f32[512,512]{1,0:T(8,128)}, f32[512,512]{1,0:T(8,12...) custom-call(f32[512,512]{1,0:T(8,128)S(1)} %get-tuple-element.24.refs_0_, ...), custom_call_target="tpu_custom_call" | custom-call | tf_op jit(solution)/shard_map/pallas_call | solution.py:453

commit v2 on v0

--- a/solution.py
+++ b/solution.py
@@ -274,11 +274,16 @@
 
     update = mm_t(back, rbasis[...]).astype(BF16)
     usend[...] = update.reshape(n, SLAB, width)
-    wide = update.astype(F32)
-    part = jnp.sum(wide * wide, axis=0, keepdims=True)
-    lanes = sum(part[:, i * 128 : (i + 1) * 128] for i in range(width // 128))
     spot = (mine * xs + x) * 2 + core
-    parts[spot] = lanes
+
+    def send_parts():
+        wide = usend[...].reshape(side, width).astype(F32)
+        part = jnp.sum(wide * wide, axis=0, keepdims=True)
+        parts[spot] = sum(part[:, i * 128 : (i + 1) * 128] for i in range(width // 128))
+        for k in sorted(
+            range(1, len(sheet)), key=lambda k: -hops(k % xs, 0) - min(k // xs, groups - k // xs)
+        ):
+            send_part(sheet[k])
 
     def send_part(there):
         pltpu.make_async_remote_copy(
@@ -290,10 +295,13 @@
             device_id_type=MESH,
         ).start()
 
-    for k in sorted(range(1, len(sheet)), key=lambda k: -hops(k % xs, 0) - min(k // xs, groups - k // xs)):
-        send_part(sheet[k])
-    pl.when(core == 0)(functools.partial(send_part, sheet[0]))
+    @pl.when(core == 0)
+    def _():
+        send_parts()
+        send_part(sheet[0])
+
     fan_out(send_update, [(c, i, j) for i in range(xs) for j in far_first(zs) for c in (1, 0)])
+    pl.when(core == 1)(send_parts)
     ubuf[me] = usend[me]
 
     loads[5].wait()

time: 40.1 us -> 40 us (level)
  no operation moved by 1% of the time
where the time goes in v2:
time: 40 us; the launch traced here: 39.9 us
  Pallas kernels  39.2 us (98%)
  between operations  0.64 us (2%)
    pallas_call x1, Pallas kernels, body(): pl.pallas_call(functools.partial(exchange_kernel, n, groups, dims), out_s...  36.7 us
    pallas_call x1, Pallas kernels, body(): pl.pallas_call(functools.partial(store_kernel, dims), out_shape=[shape(fl...  2.56 us

profile of v2, /device:TPU:16, one launch (start us, length us, event | category | flops | bytes accessed | tf_op | source)
XLA Modules:
  0.0 39.9 jit_solution(2732063983461334450)
XLA Ops:
  0.6 36.7 %shard_map.144 = (f32[512,512]{1,0:T(8,128)S(1)}, f32[512,512]{1,0:T(8,128)S(1)}, f32[512,512]{1,0:T(8,128)S(1)}, f32[512,512]{1,0:T(8,128)S(1)}, bf16[512,512]{...) custom-call(s32[64]{0:T(128)} %slot_hbm.1, ...), custom_call_target="tpu_custom_call" | custom-call | tf_op jit(solution)/shard_map/pallas_call | solution.py:410
  37.3 2.6 %shard_map.145 = (bf16[128,2048]{1,0:T(8,128)(2,1)}, f32[512,512]{1,0:T(8,128)}, f32[512,512]{1,0:T(8,128)}, f32[512,512]{1,0:T(8,128)}, f32[512,512]{1,0:T(8,12...) custom-call(f32[512,512]{1,0:T(8,128)S(1)} %get-tuple-element.24.refs_0_, ...), custom_call_target="tpu_custom_call" | custom-call | tf_op jit(solution)/shard_map/pallas_call | solution.py:461
